TPU v7x, 768 devices: a whole 4x8x12 slice. The times are simulated.
768 devices in a mesh: row: 2 (over core), col: 96 (over z, y), layer: 4 (over x).
Axes of the slice: x: 4, y: 8, z: 12, core: 2. Of those that a mesh axis runs over, the one named last changes fastest.
Arguments:
- p_tiles: bfloat16 [1536, 16, 128, 128], P(('row', 'col')), may hold values from -0.8984375 to 0.8984375
- p_offs: int32 [1536, 16], replicated, may hold values from -8 to 8, as said below
- out_offs: int32 [1536, 4], P(('row', 'col')), may hold values from -16 to 16, as said below
Outputs:
- c_tiles: bfloat16 [1536, 4, 128, 128], P(('row', 'col'), 'layer')
Inputs may be any that keep to these rules, and one draw needn't show every extreme that they name: `p_offs`: each row holds 16 distinct offsets. `out_offs`: each row holds 4 distinct offsets.
All inputs are finite; a program needn't handle non-finite values.
Results may differ from a plain program's by a relative error of at most 0.001.
Values may be sent and summed in bfloat16 or wider, within the bound.
No kernel may reach another device: no remote copies, remote signals or barrier semaphores. Data moves between devices by JAX's collectives and lax.ppermute only.
A program may use at most 64 MiB of HBM per device.

v0:
```python
import jax
import jax.numpy as jnp
from jax import lax
from jax.sharding import PartitionSpec as P

HB = 8


def passed_along(block, axis, distance):
    devices = range(lax.axis_size(axis))
    route = [((i - distance) % len(devices), i) for i in devices]
    return lax.ppermute(block, axis, route)


def pick_rows(tiles, wanted, valid):
    limit = tiles.shape[0] - 1
    chosen = jnp.take(tiles, jnp.clip(wanted, 0, limit), axis=0)
    return jnp.where(valid[:, None, None, None], chosen, jnp.zeros((), jnp.bfloat16))


def body(p_tiles, p_offs, out_offs):
    block_rows = p_tiles.shape[0]
    whole_rows = p_offs.shape[0]
    layers = lax.axis_size("layer")
    layer_now = lax.axis_index("layer")
    place = lax.axis_index(("row", "col"))
    local_offs = lax.dynamic_slice_in_dim(p_offs, place * block_rows, block_rows, 0)
    position = jnp.arange(block_rows, dtype=jnp.int32)
    per_layer = (block_rows + 2 * HB) // layers
    picks = layer_now * per_layer + jnp.arange(per_layer, dtype=jnp.int32)
    below_at = block_rows - HB + picks
    outgoing_low = pick_rows(p_tiles, below_at, picks < HB)
    from_left = passed_along(outgoing_low, ("row", "col"), 1)
    above_at = picks - block_rows - HB
    outgoing_high = pick_rows(p_tiles, above_at, above_at >= 0)
    from_right = passed_along(outgoing_high, ("row", "col"), -1)
    inner_at = picks - HB
    local_part = pick_rows(p_tiles, inner_at, (inner_at >= 0) & (inner_at < block_rows))
    needed_rows = from_left + local_part + from_right
    global_rows = (place * block_rows - HB + picks) % whole_rows
    needed_offs = p_offs[global_rows]

    def one_row(row_index):
        distance = picks - HB - row_index
        row_offsets = lax.dynamic_index_in_dim(local_offs, row_index, 0, keepdims=False)
        row_left = lax.dynamic_index_in_dim(p_tiles, row_index, 0, keepdims=False)
        row_out = lax.dynamic_index_in_dim(out_offs, row_index, 0, keepdims=False)
        select_left = (row_offsets[None, :] == distance[:, None]).astype(jnp.bfloat16)
        left_tiles = jnp.einsum(
            "kn,nab->kab", select_left, row_left, preferred_element_type=jnp.float32
        ).astype(jnp.bfloat16)
        matches = (
            distance[:, None, None] + needed_offs[:, :, None] == row_out[None, None, :]
        ).astype(jnp.bfloat16)
        chosen = jnp.einsum(
            "kms,kmab->ksab", matches, needed_rows, preferred_element_type=jnp.float32
        ).astype(jnp.bfloat16)
        return jnp.einsum("kab,ksbc->sac", left_tiles, chosen, preferred_element_type=jnp.float32)

    partial_value = lax.map(one_row, position)
    result_block = lax.psum_scatter(partial_value, "layer", scatter_dimension=1, tiled=True)
    return result_block.astype(jnp.bfloat16)


def solution(mesh):
    return jax.shard_map(
        body,
        mesh=mesh,
        in_specs=(P(("row", "col"), None, None, None), P(), P(("row", "col"), None)),
        out_specs=P(("row", "col"), "layer", None, None),
        check_vma=False,
    )
```

profile of v0, /device:TPU:1, one launch (start us, length us, event | category | flops | bytes accessed | tf_op | source)
XLA Modules:
  0.0 266.7 jit_solution(12981676418735334980)
XLA Ops:
  0.0 3.3 %gather_fusion.1 = bf16[6,16,128,128]{3,2,1,0:T(8,128)(2,1)S(1)} fusion(bf16[8,16,128,128]{3,2,1,0:T(8,128)(2,1)} %param.7, s32[1024]{0:T(1024)S(1)} %pad_clamp_fusion.2), kind=kCustom, calls=%fused_computation.clone | custom fusion | bytes 6291480 | tf_op jit(solution)/shard_map/jit(_take)/gather | solution.py:17
  3.4 2.1 select_select_fusion.2
  5.5 4.0 %collective-permute-start = (bf16[6,16,128,128]{3,2,1,0:T(8,128)(2,1)}, bf16[6,16,128,128]{3,2,1,0:T(8,128)(2,1)}, u32[]{:S(2)}, u32[]{:S(2)}) collective-permute-start(bf16[6,16,128,128]{3,2,1,0:T(8,128)(2,1)} %select_select_fusion.2), channel_id=1, source_target_pairs={{764,0},{0,4},{4,8},{8,12},{12,16},{16,20},{20,24},{24,28},{28,32}... | collective-permute-start | bytes 9437192 | tf_op jit(solution)/shard_map/ppermute | solution.py:12
  9.6 3.3 %gather_fusion.3 = bf16[6,16,128,128]{3,2,1,0:T(8,128)(2,1)S(1)} fusion(bf16[8,16,128,128]{3,2,1,0:T(8,128)(2,1)} %param.7, s32[1024]{0:T(1024)S(1)} %pad_clamp_fusion), kind=kCustom, calls=%fused_computation.2.clone | custom fusion | bytes 6291480 | tf_op jit(solution)/shard_map/jit(_take)/gather | solution.py:17
  12.9 2.1 select_select_fusion
  15.0 16.5 %collective-permute-start.1 = (bf16[6,16,128,128]{3,2,1,0:T(8,128)(2,1)}, bf16[6,16,128,128]{3,2,1,0:T(8,128)(2,1)S(1)}, u32[]{:S(2)}, u32[]{:S(2)}) collective-permute-start(bf16[6,16,128,128]{3,2,1,0:T(8,128)(2,1)} %select_select_fusion), channel_id=1, source_target_pairs={{4,0},{8,4},{12,8},{16,12},{20,16},{24,20},{28,24},{32,28},{36,32}... | collective-permute-start | bytes 9437192 | tf_op jit(solution)/shard_map/ppermute | solution.py:12
  31.5 5.0 %gather_fusion.2 = bf16[6,16,128,128]{3,2,1,0:T(8,128)(2,1)} fusion(bf16[8,16,128,128]{3,2,1,0:T(8,128)(2,1)} %param.7, s32[1024]{0:T(1024)S(1)} %pad_clamp_fusion.1), kind=kCustom, calls=%fused_computation.1.clone | custom fusion | bytes 6291480 | tf_op jit(solution)/shard_map/jit(_take)/gather | solution.py:17
  37.8 1.7 gather_fusion
  39.5 1.3 dynamic-slice
  41.4 50.7 %collective-permute-done = bf16[6,16,128,128]{3,2,1,0:T(8,128)(2,1)} collective-permute-done((bf16[6,16,128,128]{3,2,1,0:T(8,128)(2,1)}, bf16[6,16,128,128]{3,2,1,0:T(8,128)(2,1)}, u32[]{:S(2)}, u32[]{:S(2)}) %collective-permute-start) | collective-permute-done | bytes 3145760 | tf_op jit(solution)/shard_map/ppermute | solution.py:12
  92.2 7.5 %collective-permute-done.1 = bf16[6,16,128,128]{3,2,1,0:T(8,128)(2,1)S(1)} collective-permute-done((bf16[6,16,128,128]{3,2,1,0:T(8,128)(2,1)}, bf16[6,16,128,128]{3,2,1,0:T(8,128)(2,1)S(1)}, u32[]{:S(2)}, u32[]{:S(2)}) %collective-permute-start.1) | collective-permute-done | bytes 3145760 | tf_op jit(solution)/shard_map/ppermute | solution.py:12
  99.7 1.7 copy-done
  101.3 4.3 %fusion.21 = bf16[6,16,128,128]{3,2,1,0:T(8,128)(2,1)S(1)} fusion(bf16[6,16,128,128]{3,2,1,0:T(8,128)(2,1)} %copy-done, bf16[6,16,128,128]{3,2,1,0:T(8,128)(2,1)} %collective-permute-done, bf16[6,16,128,128]{3,2,1,0:T(8,128)(2,1)} %gather_fusion.2, pred[6]{0:T(512)(128)(4,1)S(1)} %get-tuple-element.179, pred[6]{0:T(512)(128)(4,1)S(1)} %get-tuple-element.180), kind=kLoop, calls=%fused_computation.33 | loop fusion | flops 6291456 | bytes 12582924 | tf_op jit(solution)/shard_map/add | solution.py:39
  105.7 117.0 %while.13 = (s32[]{:T(128)}, f32[8,4,128,128]{3,2,1,0:T(8,128)}, s32[8]{0:T(128)S(1)}, s32[6,16]{1,0:T(8,128)S(1)}, s32[8,4]{1,0:T(8,128)S(1)}, /*index=5*/bf16[...) while((s32[]{:T(128)}, f32[8,4,128,128]{3,2,1,0:T(8,128)}, ...), condition=%wide.region_1.3_spmd.clone, body=%wide.region_0.2_spmd.clone.sunk | while | flops 116392536 | bytes 9570415 | solution.py:60
  111.2 2.9 %fusion.47 = bf16[6,4,128,128]{3,1,2,0:T(4,128)(2,1)} fusion(bf16[6,16,128,128]{3,2,1,0:T(8,128)(2,1)S(1)} %get-tuple-element.267, s32[4]{0:T(128)S(1)} %fusion.45, s32[6,16]{1,0:T(8,128)S(1)} %broadcast_add_fusion.2), kind=kOutput, calls=%fused_computation.5.clone.1 | convolution fusion | flops 12583296 | bytes 3932560 | tf_op jit(solution)/shard_map/while/body/eval_jaxpr/kms,kmab->ksab/dot_general | solution.py:55
  114.1 2.2 copy.38
  116.2 1.5 convolution_bitcast_fusion.2
  118.6 1.7 constant_dynamic-update-slice_fusion.2
  125.8 2.9 %fusion.47 = bf16[6,4,128,128]{3,1,2,0:T(4,128)(2,1)} fusion(bf16[6,16,128,128]{3,2,1,0:T(8,128)(2,1)S(1)} %get-tuple-element.267, s32[4]{0:T(128)S(1)} %fusion.45, s32[6,16]{1,0:T(8,128)S(1)} %broadcast_add_fusion.2), kind=kOutput, calls=%fused_computation.5.clone.1 | convolution fusion | flops 12583296 | bytes 3932560 | tf_op jit(solution)/shard_map/while/body/eval_jaxpr/kms,kmab->ksab/dot_general | solution.py:55
  128.7 2.2 copy.38
  130.9 1.5 convolution_bitcast_fusion.2
  133.3 1.7 constant_dynamic-update-slice_fusion.2
  140.4 2.9 %fusion.47 = bf16[6,4,128,128]{3,1,2,0:T(4,128)(2,1)} fusion(bf16[6,16,128,128]{3,2,1,0:T(8,128)(2,1)S(1)} %get-tuple-element.267, s32[4]{0:T(128)S(1)} %fusion.45, s32[6,16]{1,0:T(8,128)S(1)} %broadcast_add_fusion.2), kind=kOutput, calls=%fused_computation.5.clone.1 | convolution fusion | flops 12583296 | bytes 3932560 | tf_op jit(solution)/shard_map/while/body/eval_jaxpr/kms,kmab->ksab/dot_general | solution.py:55
  143.3 2.2 copy.38
  145.5 1.6 convolution_bitcast_fusion.2
  147.9 1.7 constant_dynamic-update-slice_fusion.2
  155.1 2.9 %fusion.47 = bf16[6,4,128,128]{3,1,2,0:T(4,128)(2,1)} fusion(bf16[6,16,128,128]{3,2,1,0:T(8,128)(2,1)S(1)} %get-tuple-element.267, s32[4]{0:T(128)S(1)} %fusion.45, s32[6,16]{1,0:T(8,128)S(1)} %broadcast_add_fusion.2), kind=kOutput, calls=%fused_computation.5.clone.1 | convolution fusion | flops 12583296 | bytes 3932560 | tf_op jit(solution)/shard_map/while/body/eval_jaxpr/kms,kmab->ksab/dot_general | solution.py:55
  158.0 2.2 copy.38
  160.1 1.5 convolution_bitcast_fusion.2
  162.5 1.7 constant_dynamic-update-slice_fusion.2
  169.7 2.9 %fusion.47 = bf16[6,4,128,128]{3,1,2,0:T(4,128)(2,1)} fusion(bf16[6,16,128,128]{3,2,1,0:T(8,128)(2,1)S(1)} %get-tuple-element.267, s32[4]{0:T(128)S(1)} %fusion.45, s32[6,16]{1,0:T(8,128)S(1)} %broadcast_add_fusion.2), kind=kOutput, calls=%fused_computation.5.clone.1 | convolution fusion | flops 12583296 | bytes 3932560 | tf_op jit(solution)/shard_map/while/body/eval_jaxpr/kms,kmab->ksab/dot_general | solution.py:55
  172.6 2.2 copy.38
  174.8 1.5 convolution_bitcast_fusion.2
  177.2 1.7 constant_dynamic-update-slice_fusion.2
  184.3 2.9 %fusion.47 = bf16[6,4,128,128]{3,1,2,0:T(4,128)(2,1)} fusion(bf16[6,16,128,128]{3,2,1,0:T(8,128)(2,1)S(1)} %get-tuple-element.267, s32[4]{0:T(128)S(1)} %fusion.45, s32[6,16]{1,0:T(8,128)S(1)} %broadcast_add_fusion.2), kind=kOutput, calls=%fused_computation.5.clone.1 | convolution fusion | flops 12583296 | bytes 3932560 | tf_op jit(solution)/shard_map/while/body/eval_jaxpr/kms,kmab->ksab/dot_general | solution.py:55
  187.2 2.2 copy.38
  189.4 1.6 convolution_bitcast_fusion.2
  191.8 1.7 constant_dynamic-update-slice_fusion.2
  198.9 2.9 %fusion.47 = bf16[6,4,128,128]{3,1,2,0:T(4,128)(2,1)} fusion(bf16[6,16,128,128]{3,2,1,0:T(8,128)(2,1)S(1)} %get-tuple-element.267, s32[4]{0:T(128)S(1)} %fusion.45, s32[6,16]{1,0:T(8,128)S(1)} %broadcast_add_fusion.2), kind=kOutput, calls=%fused_computation.5.clone.1 | convolution fusion | flops 12583296 | bytes 3932560 | tf_op jit(solution)/shard_map/while/body/eval_jaxpr/kms,kmab->ksab/dot_general | solution.py:55
  201.8 2.2 copy.38
  204.0 1.5 convolution_bitcast_fusion.2
  206.4 1.7 constant_dynamic-update-slice_fusion.2
  213.5 2.9 %fusion.47 = bf16[6,4,128,128]{3,1,2,0:T(4,128)(2,1)} fusion(bf16[6,16,128,128]{3,2,1,0:T(8,128)(2,1)S(1)} %get-tuple-element.267, s32[4]{0:T(128)S(1)} %fusion.45, s32[6,16]{1,0:T(8,128)S(1)} %broadcast_add_fusion.2), kind=kOutput, calls=%fused_computation.5.clone.1 | convolution fusion | flops 12583296 | bytes 3932560 | tf_op jit(solution)/shard_map/while/body/eval_jaxpr/kms,kmab->ksab/dot_general | solution.py:55
  216.4 2.2 copy.38
  218.6 1.6 convolution_bitcast_fusion.2
  221.0 1.6 constant_dynamic-update-slice_fusion.2
  222.6 42.7 %all-reduce.2 = bf16[8,4,128,128]{3,2,1,0:T(8,128)(2,1)S(1)} all-reduce(f32[8,4,128,128]{3,2,1,0:T(8,128)} %get-tuple-element.119), channel_id=2, replica_groups=mesh['row'=2,'col'=96,'layer'=4] {'layer'}, use_global_device_ids=true, to_apply=%region_2.4.clone | all-reduce | flops 524288 | bytes 3145728
  265.3 1.3 dynamic-slice_convert_fusion
  (85 shorter events, 36.8 us)
Async XLA Ops:
  5.5 86.7 %collective-permute-start = (bf16[6,16,128,128]{3,2,1,0:T(8,128)(2,1)}, bf16[6,16,128,128]{3,2,1,0:T(8,128)(2,1)}, u32[]{:S(2)}, u32[]{:S(2)}) collective-permute-start(bf16[6,16,128,128]{3,2,1,0:T(8,128)(2,1)} %select_select_fusion.2), channel_id=1, source_target_pairs={{764,0},{0,4},{4,8},{8,12},{12,16},{16,20},{20,24},{24,28},{28,32}... | collective-permute-start | bytes 9437192 | tf_op jit(solution)/shard_map/ppermute | solution.py:12
  15.0 84.7 %collective-permute-start.1 = (bf16[6,16,128,128]{3,2,1,0:T(8,128)(2,1)}, bf16[6,16,128,128]{3,2,1,0:T(8,128)(2,1)S(1)}, u32[]{:S(2)}, u32[]{:S(2)}) collective-permute-start(bf16[6,16,128,128]{3,2,1,0:T(8,128)(2,1)} %select_select_fusion), channel_id=1, source_target_pairs={{4,0},{8,4},{12,8},{16,12},{20,16},{24,20},{28,24},{32,28},{36,32}... | collective-permute-start | bytes 9437192 | tf_op jit(solution)/shard_map/ppermute | solution.py:12
  31.5 5.0 %copy-start.1 = (s32[1536,16]{0,1:T(8,128)S(1)}, s32[1536,16]{0,1:T(8,128)}, u32[]{:S(2)}) copy-start(s32[1536,16]{0,1:T(8,128)} %param.8) | copy-start | bytes 294916
  31.5 6.2 %copy-start.2 = (s32[8,4]{0,1:T(4,128)S(1)}, s32[8,4]{0,1:T(4,128)}, u32[]{:S(2)}) copy-start(s32[8,4]{0,1:T(4,128)} %param.9) | copy-start | bytes 388
  99.7 1.7 copy-start
where the time goes:
time: 268 us; the launch traced here: 267 us
  local copies, waits for them, and re-layouts  70.6 us (26%)
  waiting for transfers between devices  58.2 us (22%)
  matrix products  44.4 us (17%)
  blocking collectives  42.7 us (16%)
  starting transfers between devices  20.5 us (8%)
  loops' own time  15.8 us (6%)
  other arithmetic  14.4 us (5%)
    ppermute x2, waiting for transfers between devices, passed_along(): return lax.ppermute(block, axis, route)  58.2 us
    unnamed x1, blocking collectives  42.7 us
    dot_general x8, matrix products, one_row(): jnp.einsum('kms,kmab->ksab', matches, needed_rows, preferred_element_type...  23.1 us
    ppermute x2, starting transfers between devices, passed_along(): return lax.ppermute(block, axis, route)  20.5 us
    dynamic_update_slice x16, local copies, waits for them, and re-layouts, body(): partial_value = lax.map(one_row, position)  20.1 us
    dot_general x8, local copies, waits for them, and re-layouts, one_row(): jnp.einsum('kms,kmab->ksab', matches, needed_rows, preferred_element_type...  17.5 us
    another operation x1, loops' own time, body(): partial_value = lax.map(one_row, position)  15.8 us
    dot_general x8, matrix products, one_row(): jnp.einsum('kab,ksbc->sac', left_tiles, chosen, preferred_element_type=jn...  12.4 us
  transfers between devices with their start and end apart: 2, of which 2 were waited for; matrix products, arithmetic and copies ran while one was open for 6% of the time, Pallas kernels for 0%

commit v1 on v0

v1 whole, which is shorter than its diff:
```python
import jax
import jax.numpy as jnp
from jax import lax
from jax.experimental import pallas as pl
from jax.experimental.pallas import tpu as pltpu
from jax.sharding import PartitionSpec as P

HB = 8
GROUP = ("row", "col")
SMEM = pltpu.SMEM
VMEM = pltpu.VMEM

BELOW = [(i, k) for i in range(8) for k in range(8) if i <= k]
ABOVE = [(i, k) for i in range(8) for k in range(8) if i >= k]


def passed_along(block, distance):
    devices = range(lax.axis_size(GROUP))
    route = [((i - distance) % len(devices), i) for i in devices]
    return lax.ppermute(block, GROUP, route)


def read_offs(p_offs, offs, sems, first):
    blocks = p_offs.shape[1] // 128
    block = first // 128
    return [
        pltpu.make_async_copy(
            p_offs.at[:, pl.ds(pl.multiple_of(lax.rem(block + part, blocks) * 128, 128), 128)],
            offs.at[part],
            sems.at[part],
        )
        for part in range(2)
    ]


def fill_table(table, offs, first, rows, nz, empty):
    start = lax.rem(first, 128)
    for r in range(rows):
        part, lane = (start + r) // 128, lax.rem(start + r, 128)
        for o in range(2 * HB + 1):
            table[r, o] = jnp.int32(empty)
        for m in range(nz):
            table[r, offs[part, m, lane] + HB] = jnp.int32(m)


def slot(table, row, offset):
    return table[row, jnp.clip(offset + HB, 0, 2 * HB)]


def send_kernel(p_offs, from_left, from_right, p_tiles, to_right, to_left, offs, table, sems):
    rows, nz = p_tiles.shape[0], p_tiles.shape[1]
    place = lax.axis_index(GROUP)
    layer = lax.axis_index("layer")
    first = place * rows
    copies = read_offs(p_offs, offs, sems, first)
    for copy in copies:
        copy.start()
    for copy in copies:
        copy.wait()
    fill_table(table, offs, first, rows, nz, 0)
    for at, (i, k) in enumerate(BELOW):
        m = slot(table, k, from_right[layer, i] - (k - rows - i))
        pltpu.make_async_copy(p_tiles.at[k, m], to_right.at[at], sems.at[2]).start()
    for at, (i, k) in enumerate(ABOVE):
        m = slot(table, k, from_left[layer, i] - (k + rows - i))
        pltpu.make_async_copy(p_tiles.at[k, m], to_left.at[at], sems.at[3]).start()
    pltpu.make_async_copy(to_right, to_right, sems.at[2]).wait()
    pltpu.make_async_copy(to_left, to_left, sems.at[3]).wait()


def own_kernel(p_offs, out_offs, p_tiles, total, left_at, offs, table, tiles, sems):
    rows, nz = p_tiles.shape[0], p_tiles.shape[1]
    whole = p_offs.shape[1]
    none = rows * nz
    place = lax.axis_index(GROUP)
    layer = lax.axis_index("layer")
    big = [
        pltpu.make_async_copy(p_tiles.at[r], tiles.at[pl.ds(r * nz, nz)], sems.at[2 + r]) for r in range(rows)
    ]
    first = lax.rem(place * rows + whole - rows, whole)
    copies = read_offs(p_offs, offs, sems, first)
    for copy in copies:
        copy.start()
    for copy in big:
        copy.start()
    tiles[none] = jnp.zeros(tiles.shape[1:], tiles.dtype)
    for copy in copies:
        copy.wait()
    fill_table(table, offs, first, 3 * rows, nz, nz)

    def left_slot(i, part, k):
        distance = k + (part - 1) * rows - i
        out = out_offs[layer, i] - distance
        m = slot(table, part * rows + k, out)
        n = slot(table, rows + i, distance)
        good = (n < nz) & (m < nz) & (out >= -HB) & (out <= HB)
        return jnp.where(good, i * nz + n, none), jnp.where(good, k * nz + m, none)

    for at, (i, k) in enumerate(BELOW):
        left_at[0, at] = left_slot(i, 0, k)[0]
    for at, (i, k) in enumerate(ABOVE):
        left_at[1, at] = left_slot(i, 2, k)[0]
    for copy in big:
        copy.wait()
    for i in range(rows):
        at = [left_slot(i, 1, k) for k in range(rows)]
        left = jnp.concatenate([tiles[a] for a, _ in at], axis=1)
        right = jnp.concatenate([tiles[b] for _, b in at], axis=0)
        total[i] = jnp.dot(left, right, preferred_element_type=jnp.float32)


def halo_kernel(left_at, p_tiles, total, below, above, out, tiles, sems):
    rows, nz = p_tiles.shape[0], p_tiles.shape[1]
    none = rows * nz
    big = [
        pltpu.make_async_copy(p_tiles.at[r], tiles.at[pl.ds(r * nz, nz)], sems.at[r]) for r in range(rows)
    ]
    for copy in big:
        copy.start()
    tiles[none] = jnp.zeros(tiles.shape[1:], tiles.dtype)
    for i in range(rows):
        big[i].wait()
        ats = [(0, at) for at, (a, _) in enumerate(BELOW) if a == i] + [(1, at) for at, (a, _) in enumerate(ABOVE) if a == i]
        left = jnp.concatenate([tiles[left_at[s, at]] for s, at in ats], axis=1)
        right = jnp.concatenate([(below, above)[s][at] for s, at in ats], axis=0)
        out[i, 0] = (total[i] + jnp.dot(left, right, preferred_element_type=jnp.float32)).astype(out.dtype)


def body(p_tiles, p_offs, out_offs):
    rows, nz, tb, _ = p_tiles.shape
    pairs = len(BELOW)
    any_spec = pl.BlockSpec(memory_space=pl.ANY)
    smem_spec = pl.BlockSpec(memory_space=SMEM)
    vmem_spec = pl.BlockSpec(memory_space=VMEM)
    limit = pltpu.CompilerParams(vmem_limit_bytes=32 << 20)
    p_offs, out_offs = p_offs.T, out_offs.T
    from_left = passed_along(out_offs, 1)
    from_right = passed_along(out_offs, -1)
    sent = jax.ShapeDtypeStruct((pairs, tb, tb), p_tiles.dtype)
    to_right, to_left = pl.pallas_call(
        send_kernel,
        out_shape=(sent, sent),
        in_specs=[any_spec, smem_spec, smem_spec, any_spec],
        out_specs=(any_spec, any_spec),
        scratch_shapes=[
            SMEM((2, nz, 128), jnp.int32),
            SMEM((rows, 2 * HB + 1), jnp.int32),
            pltpu.SemaphoreType.DMA((4,)),
        ],
        compiler_params=limit,
        name="pick_halo",
    )(p_offs, from_left, from_right, p_tiles)
    below = passed_along(to_right, 1)
    above = passed_along(to_left, -1)
    total, left_at = pl.pallas_call(
        own_kernel,
        out_shape=(
            jax.ShapeDtypeStruct((rows, tb, tb), jnp.float32),
            jax.ShapeDtypeStruct((2, pairs), jnp.int32),
        ),
        in_specs=[any_spec, smem_spec, any_spec],
        out_specs=(vmem_spec, smem_spec),
        scratch_shapes=[
            SMEM((2, nz, 128), jnp.int32),
            SMEM((3 * rows, 2 * HB + 1), jnp.int32),
            VMEM((rows * nz + 1, tb, tb), p_tiles.dtype),
            pltpu.SemaphoreType.DMA((2 + rows,)),
        ],
        compiler_params=limit,
        cost_estimate=pl.CostEstimate(flops=2 * 64 * tb**3, bytes_accessed=4 << 20, transcendentals=0),
        name="own_rows",
    )(p_offs, out_offs, p_tiles)
    return pl.pallas_call(
        halo_kernel,
        out_shape=jax.ShapeDtypeStruct((rows, 1, tb, tb), p_tiles.dtype),
        in_specs=[smem_spec, any_spec, vmem_spec, vmem_spec, vmem_spec],
        out_specs=vmem_spec,
        scratch_shapes=[
            VMEM((rows * nz + 1, tb, tb), p_tiles.dtype),
            pltpu.SemaphoreType.DMA((rows,)),
        ],
        compiler_params=limit,
        name="halo_rows",
    )(left_at, p_tiles, total, below, above)


def solution(mesh):
    return jax.shard_map(
        body,
        mesh=mesh,
        in_specs=(P(GROUP, None, None, None), P(), P(GROUP, None)),
        out_specs=P(GROUP, "layer", None, None),
        check_vma=False,
    )
```

time: 268 us -> 69.7 us (0.26)
  local copies, waits for them, and re-layouts: 70.6 us -> 3.09 us
  matrix products: 44.4 us -> 0 us
  blocking collectives: 42.7 us -> 0 us
  waiting for transfers between devices: 58.2 us -> 21.5 us
  loops' own time: 15.8 us -> 0 us
  Pallas kernels: 0 us -> 14.9 us
  other arithmetic: 14.4 us -> 0 us
  starting transfers between devices: 20.5 us -> 29.9 us
    dot_general x24 -> x0, matrix products: 44.4 us -> none  [the longest x8 23.1 us: one_row(): jnp.einsum('kms,kmab->ksab', matches, needed_rows, preferred_element_type...]
    unnamed x1 -> x0, blocking collectives: 42.7 us -> none
    ppermute x2 -> x4, waiting for transfers between devices: 58.2 us -> 21.5 us  [passed_along(): return lax.ppermute(block, GROUP, route)]
    dynamic_update_slice x16 -> x0, local copies, waits for them, and re-layouts: 20.1 us -> none  [body(): partial_value = lax.map(one_row, position)]
    dot_general x8 -> x0, local copies, waits for them, and re-layouts: 17.5 us -> none  [one_row(): jnp.einsum('kms,kmab->ksab', matches, needed_rows, preferred_element_type...]
    another operation x1 -> x0, loops' own time: 15.8 us -> none  [body(): partial_value = lax.map(one_row, position)]
    pallas_call x0 -> x3, Pallas kernels: none -> 14.9 us  [the longest x1 6.42 us: body(): pl.pallas_call(send_kernel, out_shape=(sent, sent), in_specs=[any_spec, s...]
    gather x4 -> x0, local copies, waits for them, and re-layouts: 13.4 us -> none  [the longest x3 11.7 us: pick_rows(): chosen = jnp.take(tiles, jnp.clip(wanted, 0, limit), axis=0)]
  transfers between devices with their start and end apart: 2 -> 4, of which waited for: 2 -> 3; matrix products, arithmetic and copies ran while one was open for 6% -> 0% of each run, Pallas kernels for 0% -> 7%
where the time goes in v1:
time: 69.7 us; the launch traced here: 69.5 us
  starting transfers between devices  29.9 us (43%)
  waiting for transfers between devices  21.5 us (31%)
  Pallas kernels  14.9 us (21%)
  local copies, waits for them, and re-layouts  3.09 us (4%)
    ppermute x4, starting transfers between devices, passed_along(): return lax.ppermute(block, GROUP, route)  29.9 us
    ppermute x4, waiting for transfers between devices, passed_along(): return lax.ppermute(block, GROUP, route)  21.5 us
    pallas_call x1, Pallas kernels, body(): pl.pallas_call(send_kernel, out_shape=(sent, sent), in_specs=[any_spec, s...  6.42 us
    pallas_call x1, Pallas kernels, body(): pl.pallas_call(own_kernel, out_shape=(jax.ShapeDtypeStruct((rows, tb, tb)...  4.86 us
    pallas_call x1, Pallas kernels, body(): pl.pallas_call(halo_kernel, out_shape=jax.ShapeDtypeStruct((rows, 1, tb,...  3.59 us
    unnamed x8, local copies, waits for them, and re-layouts  3.09 us
  transfers between devices with their start and end apart: 4, of which 3 were waited for; matrix products, arithmetic and copies ran while one was open for 0% of the time, Pallas kernels for 7%

profile of v1, /device:TPU:1, one launch (start us, length us, event | category | flops | bytes accessed | tf_op | source)
XLA Modules:
  0.0 69.5 jit_solution(5759605262878229989)
XLA Ops:
  0.0 4.0 %collective-permute-start = (s32[4,8]{1,0:T(4,128)}, s32[4,8]{1,0:T(4,128)S(1)}, u32[]{:S(2)}, u32[]{:S(2)}) collective-permute-start(s32[4,8]{1,0:T(4,128)} %bitcast.4), channel_id=1, source_target_pairs={{764,0},{0,4},{4,8},{8,12},{12,16},{16,20},{20,24},{24,28},{28,32}... | collective-permute-start | bytes 392 | tf_op jit(solution)/shard_map/ppermute | solution.py:20
  4.0 16.5 %collective-permute-start.1 = (s32[4,8]{1,0:T(4,128)}, s32[4,8]{1,0:T(4,128)S(1)}, u32[]{:S(2)}, u32[]{:S(2)}) collective-permute-start(s32[4,8]{1,0:T(4,128)} %bitcast.5), channel_id=1, source_target_pairs={{4,0},{8,4},{12,8},{16,12},{20,16},{24,20},{28,24},{32,28},{36,32}... | collective-permute-start | bytes 392 | tf_op jit(solution)/shard_map/ppermute | solution.py:20
  20.5 0.0 collective-permute-done.from_left
  20.5 0.9 %collective-permute-done.1.from_right = s32[4,8]{1,0:T(4,128)S(1)} collective-permute-done((s32[4,8]{1,0:T(4,128)}, s32[4,8]{1,0:T(4,128)S(1)}, u32[]{:S(2)}, u32[]{:S(2)}) %collective-permute-start.1) | collective-permute-done | bytes 160 | tf_op jit(solution)/shard_map/ppermute | solution.py:20
  21.4 0.0 copy-start
  21.5 2.2 %copy-done = bf16[8,16,128,128]{3,2,1,0:T(8,128)(2,1)S(1)} copy-done((bf16[8,16,128,128]{3,2,1,0:T(8,128)(2,1)S(1)}, bf16[8,16,128,128]{3,2,1,0:T(8,128)(2,1)}, u32[]{:S(2)}) %copy-start) | copy-done | bytes 4194328
  23.6 0.0 copy-start.2
  23.6 0.9 %copy-done.2 = s32[1536,16]{0,1:T(8,128)S(1)} copy-done((s32[1536,16]{0,1:T(8,128)S(1)}, s32[1536,16]{0,1:T(8,128)}, u32[]{:S(2)}) %copy-start.2) | copy-done | bytes 98328
  24.5 0.0 copy-start.1
  24.5 0.0 copy-start.3
  24.5 6.4 %pick_halo.1 = (bf16[36,128,128]{2,1,0:T(8,128)(2,1)S(1)}, bf16[36,128,128]{2,1,0:T(8,128)(2,1)S(1)}) custom-call(s32[16,1536]{1,0:T(8,128)S(1)} %bitcast.2, s32[4,8]{1,0:T(4,128)S(1)} %collective-permute-done.from_left, s32[4,8]{1,0:T(4,128)S(1)} %collective-permute-done.1.from_right, bf16[8,16,128,128]{3,2,1,0:T(8,128)(2,1)S(1)} %copy-done), custom_call_target="tpu_custom_call" | custom-call | tf_op jit(solution)/shard_map/pick_halo/pallas_call | solution.py:140
  31.0 1.9 %collective-permute-start.2 = (bf16[36,128,128]{2,1,0:T(8,128)(2,1)S(1)}, bf16[36,128,128]{2,1,0:T(8,128)(2,1)S(1)}, u32[]{:S(2)}, u32[]{:S(2)}) collective-permute-start(bf16[36,128,128]{2,1,0:T(8,128)(2,1)S(1)} %get-tuple-element.11), channel_id=1, source_target_pairs={{764,0},{0,4},{4,8},{8,12},{12,16},{16,20},{20,24},{24,28},{28,32}... | collective-permute-start | bytes 3538952 | tf_op jit(solution)/shard_map/ppermute | solution.py:20
  32.9 7.5 %collective-permute-start.3 = (bf16[36,128,128]{2,1,0:T(8,128)(2,1)S(1)}, bf16[36,128,128]{2,1,0:T(8,128)(2,1)S(1)}, u32[]{:S(2)}, u32[]{:S(2)}) collective-permute-start(bf16[36,128,128]{2,1,0:T(8,128)(2,1)S(1)} %get-tuple-element.12), channel_id=1, source_target_pairs={{4,0},{8,4},{12,8},{16,12},{20,16},{24,20},{28,24},{32,28},{36,32}... | collective-permute-start | bytes 3538952 | tf_op jit(solution)/shard_map/ppermute | solution.py:20
  40.4 0.0 copy-done.1
  40.4 0.0 copy-done.3
  40.4 4.9 %own_rows.1 = (f32[8,128,128]{2,1,0:T(8,128)S(1)}, s32[2,36]{1,0:T(2,128)S(1)}) custom-call(s32[16,1536]{1,0:T(8,128)S(1)} %bitcast.3, s32[4,8]{1,0:T(4,128)S(1)} %bitcast.6, bf16[8,16,128,128]{3,2,1,0:T(8,128)(2,1)S(1)} %copy-done.1), custom_call_target="tpu_custom_call" | custom-call | flops 268435456 | bytes 4194304 | tf_op jit(solution)/shard_map/own_rows/pallas_call | solution.py:155
  45.3 19.1 %collective-permute-done.2.below = bf16[36,128,128]{2,1,0:T(8,128)(2,1)S(1)} collective-permute-done((bf16[36,128,128]{2,1,0:T(8,128)(2,1)S(1)}, bf16[36,128,128]{2,1,0:T(8,128)(2,1)S(1)}, u32[]{:S(2)}, u32[]{:S(2)}) %collective-permute-start.2) | collective-permute-done | bytes 1179680 | tf_op jit(solution)/shard_map/ppermute | solution.py:20
  64.4 1.5 %collective-permute-done.3.above = bf16[36,128,128]{2,1,0:T(8,128)(2,1)S(1)} collective-permute-done((bf16[36,128,128]{2,1,0:T(8,128)(2,1)S(1)}, bf16[36,128,128]{2,1,0:T(8,128)(2,1)S(1)}, u32[]{:S(2)}, u32[]{:S(2)}) %collective-permute-start.3) | collective-permute-done | bytes 1179680 | tf_op jit(solution)/shard_map/ppermute | solution.py:20
  65.9 3.6 %halo_rows.1 = bf16[8,1,128,128]{3,2,1,0:T(8,128)(2,1)} custom-call(s32[2,36]{1,0:T(2,128)S(1)} %get-tuple-element.9.left_at, bf16[8,16,128,128]{3,2,1,0:T(8,128)(2,1)S(1)} %copy-done.1, f32[8,128,128]{2,1,0:T(8,128)S(1)} %get-tuple-element.10.total, bf16[36,128,128]{2,1,0:T(8,128)(2,1)S(1)} %collective-permute-done.2.below, ...), custom_call_target="tpu_custom_call" | custom-call | tf_op jit(solution)/shard_map/halo_rows/pallas_call | solution.py:173
Async XLA Ops:
  0.0 20.5 %collective-permute-start = (s32[4,8]{1,0:T(4,128)}, s32[4,8]{1,0:T(4,128)S(1)}, u32[]{:S(2)}, u32[]{:S(2)}) collective-permute-start(s32[4,8]{1,0:T(4,128)} %bitcast.4), channel_id=1, source_target_pairs={{764,0},{0,4},{4,8},{8,12},{12,16},{16,20},{20,24},{24,28},{28,32}... | collective-permute-start | bytes 392 | tf_op jit(solution)/shard_map/ppermute | solution.py:20
  4.0 17.4 %collective-permute-start.1 = (s32[4,8]{1,0:T(4,128)}, s32[4,8]{1,0:T(4,128)S(1)}, u32[]{:S(2)}, u32[]{:S(2)}) collective-permute-start(s32[4,8]{1,0:T(4,128)} %bitcast.5), channel_id=1, source_target_pairs={{4,0},{8,4},{12,8},{16,12},{20,16},{24,20},{28,24},{32,28},{36,32}... | collective-permute-start | bytes 392 | tf_op jit(solution)/shard_map/ppermute | solution.py:20
  21.4 2.2 %copy-start = (bf16[8,16,128,128]{3,2,1,0:T(8,128)(2,1)S(1)}, bf16[8,16,128,128]{3,2,1,0:T(8,128)(2,1)}, u32[]{:S(2)}) copy-start(bf16[8,16,128,128]{3,2,1,0:T(8,128)(2,1)} %p_tiles.5) | copy-start | bytes 12582916
  23.6 0.9 %copy-start.2 = (s32[1536,16]{0,1:T(8,128)S(1)}, s32[1536,16]{0,1:T(8,128)}, u32[]{:S(2)}) copy-start(s32[1536,16]{0,1:T(8,128)} %param.4) | copy-start | bytes 294916
  24.5 15.9 %copy-start.1 = (bf16[8,16,128,128]{3,2,1,0:T(8,128)(2,1)S(1)}, bf16[8,16,128,128]{3,2,1,0:T(8,128)(2,1)}, u32[]{:S(2)}) copy-start(bf16[8,16,128,128]{3,2,1,0:T(8,128)(2,1)} %p_tiles.5) | copy-start | bytes 12582916
  24.5 15.9 %copy-start.3 = (s32[8,4]{0,1:T(4,128)S(1)}, s32[8,4]{0,1:T(4,128)}, u32[]{:S(2)}) copy-start(s32[8,4]{0,1:T(4,128)} %param.5) | copy-start | bytes 388
  31.0 33.5 %collective-permute-start.2 = (bf16[36,128,128]{2,1,0:T(8,128)(2,1)S(1)}, bf16[36,128,128]{2,1,0:T(8,128)(2,1)S(1)}, u32[]{:S(2)}, u32[]{:S(2)}) collective-permute-start(bf16[36,128,128]{2,1,0:T(8,128)(2,1)S(1)} %get-tuple-element.11), channel_id=1, source_target_pairs={{764,0},{0,4},{4,8},{8,12},{12,16},{16,20},{20,24},{24,28},{28,32}... | collective-permute-start | bytes 3538952 | tf_op jit(solution)/shard_map/ppermute | solution.py:20
  32.9 33.0 %collective-permute-start.3 = (bf16[36,128,128]{2,1,0:T(8,128)(2,1)S(1)}, bf16[36,128,128]{2,1,0:T(8,128)(2,1)S(1)}, u32[]{:S(2)}, u32[]{:S(2)}) collective-permute-start(bf16[36,128,128]{2,1,0:T(8,128)(2,1)S(1)} %get-tuple-element.12), channel_id=1, source_target_pairs={{4,0},{8,4},{12,8},{16,12},{20,16},{24,20},{28,24},{32,28},{36,32}... | collective-permute-start | bytes 3538952 | tf_op jit(solution)/shard_map/ppermute | solution.py:20

commit v2 on v0

v2 whole, which is shorter than its diff:
```python
import jax
import jax.numpy as jnp
from jax import lax
from jax.experimental import pallas as pl
from jax.experimental.pallas import tpu as pltpu
from jax.sharding import PartitionSpec as P

HB = 8
WIDTH = 2 * HB + 1
GROUP = ("row", "col")
SMEM = pltpu.SMEM
VMEM = pltpu.VMEM
ANY_SPEC = pl.BlockSpec(memory_space=pl.ANY)
SMEM_SPEC = pl.BlockSpec(memory_space=SMEM)
VMEM_SPEC = pl.BlockSpec(memory_space=VMEM)
LIMIT = pltpu.CompilerParams(vmem_limit_bytes=32 << 20)

BELOW = [(i, k) for i in range(8) for k in range(8) if i <= k]
ABOVE = [(i, k) for i in range(8) for k in range(8) if i >= k]


def passed_along(block, distance):
    devices = range(lax.axis_size(GROUP))
    route = [((i - distance) % len(devices), i) for i in devices]
    return lax.ppermute(block, GROUP, route)


def slot(table, row, offset, nz):
    found = table[row, jnp.clip(offset + HB, 0, WIDTH - 1)]
    return jnp.where((offset >= -HB) & (offset <= HB), found, nz)


def fill_table(p_offs, table, offs, sems, rows, before):
    nz, whole = p_offs.shape
    first = lax.rem(lax.axis_index(GROUP) * 8 + whole - before, whole)
    block, start = first // 128, lax.rem(first, 128)
    copies = [
        pltpu.make_async_copy(
            p_offs.at[:, pl.ds(pl.multiple_of(lax.rem(block + part, whole // 128) * 128, 128), 128)],
            offs.at[part],
            sems.at[part],
        )
        for part in range(2)
    ]
    for copy in copies:
        copy.start()
    for r in range(rows):
        for o in range(WIDTH):
            table[r, o] = jnp.int32(nz)
    for copy in copies:
        copy.wait()
    for r in range(rows):
        part, lane = (start + r) // 128, lax.rem(start + r, 128)
        found = [offs[part, m, lane] + HB for m in range(nz)]
        for m in range(nz):
            table[r, found[m]] = jnp.int32(m)


def prepare_kernel(p_offs, table, offs, sems):
    fill_table(p_offs, table, offs, sems, table.shape[0], 0)


def pick_kernel(pairs, shift, table, asked, tiles, picked):
    rows, nz = tiles.shape[0], tiles.shape[1]
    layer = lax.axis_index("layer")
    for at, (i, k) in enumerate(pairs):
        m = slot(table, k, asked[layer, i] - (k - i + shift), nz)
        picked[at] = tiles[k, jnp.minimum(m, nz - 1)]


def own_kernel(p_offs, out_offs, tiles, total, left_below, left_above, table, offs, sems):
    rows, nz = tiles.shape[0], tiles.shape[1]
    fill_table(p_offs, table, offs, sems, 3 * rows, rows)
    layer = lax.axis_index("layer")

    def pair(i, k, shift):
        distance = k + shift - i
        m = slot(table, rows + shift + k, out_offs[layer, i] - distance, nz)
        n = slot(table, rows + i, distance, nz)
        left = tiles[i, jnp.minimum(n, nz - 1)]
        return jnp.where((n < nz) & (m < nz), left, jnp.zeros_like(left)), jnp.minimum(m, nz - 1)

    for left, pairs, shift in ((left_below, BELOW, -rows), (left_above, ABOVE, rows)):
        for at, (i, k) in enumerate(pairs):
            left[at] = pair(i, k, shift)[0]
    for i in range(rows):
        at = [pair(i, k, 0) for k in range(rows)]
        left = jnp.concatenate([a for a, _ in at], axis=1)
        right = jnp.concatenate([tiles[k, m] for k, (_, m) in enumerate(at)], axis=0)
        total[i] = jnp.dot(left, right, preferred_element_type=jnp.float32)


def halo_kernel(pairs, total, left, right, out):
    for i in range(total.shape[0]):
        ats = [at for at, (a, _) in enumerate(pairs) if a == i]
        product = jnp.dot(
            jnp.concatenate([left[at] for at in ats], axis=1),
            jnp.concatenate([right[at] for at in ats], axis=0),
            preferred_element_type=jnp.float32,
        )
        out[i] = (total[i] + product).astype(out.dtype)


def cost(products, moved):
    return pl.CostEstimate(flops=2 * products * 128**3, bytes_accessed=moved, transcendentals=0)


def body(p_tiles, p_offs, out_offs):
    rows, nz, tb, _ = p_tiles.shape
    count = len(BELOW)
    dtype = p_tiles.dtype
    p_offs, out_offs = p_offs.T, out_offs.T
    offs_scratch = [SMEM((2, nz, 128), jnp.int32), pltpu.SemaphoreType.DMA((2,))]
    table = pl.pallas_call(
        prepare_kernel,
        out_shape=jax.ShapeDtypeStruct((rows, WIDTH), jnp.int32),
        in_specs=[ANY_SPEC],
        out_specs=SMEM_SPEC,
        scratch_shapes=offs_scratch,
        compiler_params=LIMIT,
        cost_estimate=cost(4000, 8 << 20),
        name="prepare",
    )(p_offs)
    from_left = passed_along(out_offs, 1)
    from_right = passed_along(out_offs, -1)
    from_left, from_right = lax.optimization_barrier((from_left, from_right))

    def pick(pairs, shift, wanted, name):
        return pl.pallas_call(
            lambda *refs: pick_kernel(pairs, shift, *refs),
            out_shape=jax.ShapeDtypeStruct((count, tb, tb), dtype),
            in_specs=[SMEM_SPEC, SMEM_SPEC, VMEM_SPEC],
            out_specs=VMEM_SPEC,
            compiler_params=LIMIT,
            cost_estimate=cost(0, 2 << 20),
            name=name,
        )(table, wanted, p_tiles)

    below = passed_along(pick(BELOW, -rows, from_right, "pick_right"), 1)
    above = passed_along(pick(ABOVE, rows, from_left, "pick_left"), -1)
    left_shape = jax.ShapeDtypeStruct((count, tb, tb), dtype)
    sum_shape = jax.ShapeDtypeStruct((rows, tb, tb), jnp.float32)
    total, left_below, left_above = pl.pallas_call(
        own_kernel,
        out_shape=(sum_shape, left_shape, left_shape),
        in_specs=[ANY_SPEC, SMEM_SPEC, VMEM_SPEC],
        out_specs=(VMEM_SPEC, VMEM_SPEC, VMEM_SPEC),
        scratch_shapes=[SMEM((3 * rows, WIDTH), jnp.int32), *offs_scratch],
        compiler_params=LIMIT,
        cost_estimate=cost(64, 8 << 20),
        name="own_rows",
    )(p_offs, out_offs, p_tiles)

    def halo(pairs, total, left, right, out_shape, name):
        return pl.pallas_call(
            lambda *refs: halo_kernel(pairs, *refs),
            out_shape=out_shape,
            in_specs=[VMEM_SPEC, VMEM_SPEC, VMEM_SPEC],
            out_specs=VMEM_SPEC,
            compiler_params=LIMIT,
            cost_estimate=cost(count, 4 << 20),
            name=name,
        )(total, left, right)

    total = halo(BELOW, total, left_below, below, sum_shape, "rows_below")
    result = halo(ABOVE, total, left_above, above, jax.ShapeDtypeStruct((rows, tb, tb), dtype), "rows_above")
    return result[:, None]


def solution(mesh):
    return jax.shard_map(
        body,
        mesh=mesh,
        in_specs=(P(GROUP, None, None, None), P(), P(GROUP, None)),
        out_specs=P(GROUP, "layer", None, None),
        check_vma=False,
    )
```

time: 268 us -> 61.5 us (0.23)
  local copies, waits for them, and re-layouts: 70.6 us -> 1.07 us
  matrix products: 44.4 us -> 0 us
  blocking collectives: 42.7 us -> 0 us
  waiting for transfers between devices: 58.2 us -> 20.5 us
  loops' own time: 15.8 us -> 0 us
  other arithmetic: 14.4 us -> 0 us
  Pallas kernels: 0 us -> 10.1 us
  starting transfers between devices: 20.5 us -> 29.4 us
    dot_general x24 -> x0, matrix products: 44.4 us -> none  [the longest x8 23.1 us: one_row(): jnp.einsum('kms,kmab->ksab', matches, needed_rows, preferred_element_type...]
    unnamed x1 -> x0, blocking collectives: 42.7 us -> none
    ppermute x2 -> x4, waiting for transfers between devices: 58.2 us -> 20.5 us  [passed_along(): return lax.ppermute(block, GROUP, route)]
    dynamic_update_slice x16 -> x0, local copies, waits for them, and re-layouts: 20.1 us -> none  [body(): partial_value = lax.map(one_row, position)]
    dot_general x8 -> x0, local copies, waits for them, and re-layouts: 17.5 us -> none  [one_row(): jnp.einsum('kms,kmab->ksab', matches, needed_rows, preferred_element_type...]
    another operation x1 -> x0, loops' own time: 15.8 us -> none  [body(): partial_value = lax.map(one_row, position)]
    gather x4 -> x0, local copies, waits for them, and re-layouts: 13.4 us -> none  [the longest x3 11.7 us: pick_rows(): chosen = jnp.take(tiles, jnp.clip(wanted, 0, limit), axis=0)]
    pallas_call x0 -> x6, Pallas kernels: none -> 10.1 us  [the longest x1 4.76 us: body(): pl.pallas_call(own_kernel, out_shape=(sum_shape, left_shape, left_shape),...]
  transfers between devices with their start and end apart: 2 -> 4, of which waited for: 2 -> 2; matrix products, arithmetic and copies ran while one was open for 6% -> 0% of each run, Pallas kernels for 0% -> 13%
where the time goes in v2:
time: 61.5 us; the launch traced here: 61.2 us
  starting transfers between devices  29.4 us (48%)
  waiting for transfers between devices  20.5 us (33%)
  Pallas kernels  10.1 us (16%)
  local copies, waits for them, and re-layouts  1.07 us (2%)
    ppermute x4, starting transfers between devices, passed_along(): return lax.ppermute(block, GROUP, route)  29.4 us
    ppermute x4, waiting for transfers between devices, passed_along(): return lax.ppermute(block, GROUP, route)  20.5 us
    pallas_call x1, Pallas kernels, body(): pl.pallas_call(own_kernel, out_shape=(sum_shape, left_shape, left_shape),...  4.76 us
    pallas_call x1, Pallas kernels, body(): pl.pallas_call(prepare_kernel, out_shape=jax.ShapeDtypeStruct((rows, WIDT...  1.98 us
    pallas_call x2, Pallas kernels, pick(): pl.pallas_call(lambda *refs: pick_kernel(pairs, shift, *refs), out_shape=...  1.69 us
    pallas_call x2, Pallas kernels, halo(): pl.pallas_call(lambda *refs: halo_kernel(pairs, *refs), out_shape=out_sha...  1.65 us
  transfers between devices with their start and end apart: 4, of which 2 were waited for; matrix products, arithmetic and copies ran while one was open for 0% of the time, Pallas kernels for 13%

profile of v2, /device:TPU:1, one launch (start us, length us, event | category | flops | bytes accessed | tf_op | source)
XLA Modules:
  0.0 61.2 jit_solution(10837984068198792013)
XLA Ops:
  0.0 4.0 %collective-permute-start = (s32[4,8]{1,0:T(4,128)}, s32[4,8]{1,0:T(4,128)S(1)}, u32[]{:S(2)}, u32[]{:S(2)}) collective-permute-start(s32[4,8]{1,0:T(4,128)} %bitcast.7), channel_id=1, source_target_pairs={{764,0},{0,4},{4,8},{8,12},{12,16},{16,20},{20,24},{24,28},{28,32}... | collective-permute-start | bytes 392 | tf_op jit(solution)/shard_map/ppermute | solution.py:25
  4.0 16.5 %collective-permute-start.1 = (s32[4,8]{1,0:T(4,128)}, s32[4,8]{1,0:T(4,128)S(1)}, u32[]{:S(2)}, u32[]{:S(2)}) collective-permute-start(s32[4,8]{1,0:T(4,128)} %bitcast.8), channel_id=1, source_target_pairs={{4,0},{8,4},{12,8},{16,12},{20,16},{24,20},{28,24},{32,28},{36,32}... | collective-permute-start | bytes 392 | tf_op jit(solution)/shard_map/ppermute | solution.py:25
  20.5 0.0 copy-start.1
  20.5 0.9 %copy-done.1 = s32[1536,16]{0,1:T(8,128)S(1)} copy-done((s32[1536,16]{0,1:T(8,128)S(1)}, s32[1536,16]{0,1:T(8,128)}, u32[]{:S(2)}) %copy-start.1) | copy-done | bytes 98328
  21.4 0.0 copy-start
  21.4 2.0 %prepare.1.refs_0_ = s32[8,17]{1,0:T(8,128)S(1)} custom-call(s32[16,1536]{1,0:T(8,128)S(1)} %bitcast.5), custom_call_target="tpu_custom_call" | custom-call | flops 16777216000 | bytes 8388608 | tf_op jit(solution)/shard_map/prepare/pallas_call | solution.py:114
  23.4 0.0 collective-permute-done.refs_1_
  23.4 0.0 collective-permute-done.1.refs_1_
  23.4 0.2 copy-done
  23.6 0.8 %pick_right.1 = bf16[36,128,128]{2,1,0:T(8,128)(2,1)S(1)} custom-call(s32[8,17]{1,0:T(8,128)S(1)} %prepare.1.refs_0_, s32[4,8]{1,0:T(4,128)S(1)} %collective-permute-done.1.refs_1_, bf16[8,16,128,128]{3,2,1,0:T(8,128)(2,1)S(1)} %copy-done), custom_call_target="tpu_custom_call" | custom-call | bytes 2097152 | tf_op jit(solution)/shard_map/pick_right/pallas_call | solution.py:129
  24.5 0.0 copy-start.2
  24.5 1.9 %collective-permute-start.2 = (bf16[36,128,128]{2,1,0:T(8,128)(2,1)S(1)}, bf16[36,128,128]{2,1,0:T(8,128)(2,1)S(1)}, u32[]{:S(2)}, u32[]{:S(2)}) collective-permute-start(bf16[36,128,128]{2,1,0:T(8,128)(2,1)S(1)} %pick_right.1), channel_id=1, source_target_pairs={{764,0},{0,4},{4,8},{8,12},{12,16},{16,20},{20,24},{24,28},{28,32}... | collective-permute-start | bytes 3538952 | tf_op jit(solution)/shard_map/ppermute | solution.py:25
  26.4 0.8 %pick_left.1 = bf16[36,128,128]{2,1,0:T(8,128)(2,1)S(1)} custom-call(s32[8,17]{1,0:T(8,128)S(1)} %prepare.1.refs_0_, s32[4,8]{1,0:T(4,128)S(1)} %collective-permute-done.refs_1_, bf16[8,16,128,128]{3,2,1,0:T(8,128)(2,1)S(1)} %copy-done), custom_call_target="tpu_custom_call" | custom-call | bytes 2097152 | tf_op jit(solution)/shard_map/pick_left/pallas_call | solution.py:129
  27.3 7.0 %collective-permute-start.3 = (bf16[36,128,128]{2,1,0:T(8,128)(2,1)S(1)}, bf16[36,128,128]{2,1,0:T(8,128)(2,1)S(1)}, u32[]{:S(2)}, u32[]{:S(2)}) collective-permute-start(bf16[36,128,128]{2,1,0:T(8,128)(2,1)S(1)} %pick_left.1), channel_id=1, source_target_pairs={{4,0},{8,4},{12,8},{16,12},{20,16},{24,20},{28,24},{32,28},{36,32}... | collective-permute-start | bytes 3538952 | tf_op jit(solution)/shard_map/ppermute | solution.py:25
  34.2 0.0 copy-done.2
  34.2 4.8 %own_rows.1 = (f32[8,128,128]{2,1,0:T(8,128)S(1)}, bf16[36,128,128]{2,1,0:T(8,128)(2,1)S(1)}, bf16[36,128,128]{2,1,0:T(8,128)(2,1)S(1)}) custom-call(s32[16,1536]{1,0:T(8,128)S(1)} %bitcast.6, s32[4,8]{1,0:T(4,128)S(1)} %bitcast.9, bf16[8,16,128,128]{3,2,1,0:T(8,128)(2,1)S(1)} %copy-done), custom_call_target="tpu_custom_call" | custom-call | flops 268435456 | bytes 8388608 | tf_op jit(solution)/shard_map/own_rows/pallas_call | solution.py:143
  39.0 18.1 %collective-permute-done.2.refs_2_ = bf16[36,128,128]{2,1,0:T(8,128)(2,1)S(1)} collective-permute-done((bf16[36,128,128]{2,1,0:T(8,128)(2,1)S(1)}, bf16[36,128,128]{2,1,0:T(8,128)(2,1)S(1)}, u32[]{:S(2)}, u32[]{:S(2)}) %collective-permute-start.2) | collective-permute-done | bytes 1179680 | tf_op jit(solution)/shard_map/ppermute | solution.py:25
  57.1 0.5 rows_below.1.refs_0_
  57.6 2.4 %collective-permute-done.3.refs_2_ = bf16[36,128,128]{2,1,0:T(8,128)(2,1)S(1)} collective-permute-done((bf16[36,128,128]{2,1,0:T(8,128)(2,1)S(1)}, bf16[36,128,128]{2,1,0:T(8,128)(2,1)S(1)}, u32[]{:S(2)}, u32[]{:S(2)}) %collective-permute-start.3) | collective-permute-done | bytes 1179680 | tf_op jit(solution)/shard_map/ppermute | solution.py:25
  60.0 1.2 %rows_above.1 = bf16[8,128,128]{2,1,0:T(8,128)(2,1)} custom-call(f32[8,128,128]{2,1,0:T(8,128)S(1)} %rows_below.1.refs_0_, bf16[36,128,128]{2,1,0:T(8,128)(2,1)S(1)} %get-tuple-element.13.refs_1_, bf16[36,128,128]{2,1,0:T(8,128)(2,1)S(1)} %collective-permute-done.3.refs_2_), custom_call_target="tpu_custom_call" | custom-call | flops 150994944 | bytes 4194304 | tf_op jit(solution)/shard_map/rows_above/pallas_call | solution.py:155
Async XLA Ops:
  0.0 23.4 %collective-permute-start = (s32[4,8]{1,0:T(4,128)}, s32[4,8]{1,0:T(4,128)S(1)}, u32[]{:S(2)}, u32[]{:S(2)}) collective-permute-start(s32[4,8]{1,0:T(4,128)} %bitcast.7), channel_id=1, source_target_pairs={{764,0},{0,4},{4,8},{8,12},{12,16},{16,20},{20,24},{24,28},{28,32}... | collective-permute-start | bytes 392 | tf_op jit(solution)/shard_map/ppermute | solution.py:25
  4.0 19.4 %collective-permute-start.1 = (s32[4,8]{1,0:T(4,128)}, s32[4,8]{1,0:T(4,128)S(1)}, u32[]{:S(2)}, u32[]{:S(2)}) collective-permute-start(s32[4,8]{1,0:T(4,128)} %bitcast.8), channel_id=1, source_target_pairs={{4,0},{8,4},{12,8},{16,12},{20,16},{24,20},{28,24},{32,28},{36,32}... | collective-permute-start | bytes 392 | tf_op jit(solution)/shard_map/ppermute | solution.py:25
  20.5 0.9 %copy-start.1 = (s32[1536,16]{0,1:T(8,128)S(1)}, s32[1536,16]{0,1:T(8,128)}, u32[]{:S(2)}) copy-start(s32[1536,16]{0,1:T(8,128)} %param.4) | copy-start | bytes 294916
  21.4 2.2 %copy-start = (bf16[8,16,128,128]{3,2,1,0:T(8,128)(2,1)S(1)}, bf16[8,16,128,128]{3,2,1,0:T(8,128)(2,1)}, u32[]{:S(2)}) copy-start(bf16[8,16,128,128]{3,2,1,0:T(8,128)(2,1)} %refs_2_.3) | copy-start | bytes 12582916
  24.5 9.8 %copy-start.2 = (s32[8,4]{0,1:T(4,128)S(1)}, s32[8,4]{0,1:T(4,128)}, u32[]{:S(2)}) copy-start(s32[8,4]{0,1:T(4,128)} %param.5) | copy-start | bytes 388
  24.5 32.6 %collective-permute-start.2 = (bf16[36,128,128]{2,1,0:T(8,128)(2,1)S(1)}, bf16[36,128,128]{2,1,0:T(8,128)(2,1)S(1)}, u32[]{:S(2)}, u32[]{:S(2)}) collective-permute-start(bf16[36,128,128]{2,1,0:T(8,128)(2,1)S(1)} %pick_right.1), channel_id=1, source_target_pairs={{764,0},{0,4},{4,8},{8,12},{12,16},{16,20},{20,24},{24,28},{28,32}... | collective-permute-start | bytes 3538952 | tf_op jit(solution)/shard_map/ppermute | solution.py:25
  27.3 32.7 %collective-permute-start.3 = (bf16[36,128,128]{2,1,0:T(8,128)(2,1)S(1)}, bf16[36,128,128]{2,1,0:T(8,128)(2,1)S(1)}, u32[]{:S(2)}, u32[]{:S(2)}) collective-permute-start(bf16[36,128,128]{2,1,0:T(8,128)(2,1)S(1)} %pick_left.1), channel_id=1, source_target_pairs={{4,0},{8,4},{12,8},{16,12},{20,16},{24,20},{28,24},{32,28},{36,32}... | collective-permute-start | bytes 3538952 | tf_op jit(solution)/shard_map/ppermute | solution.py:25

commit v3 on v2

--- a/solution.py
+++ b/solution.py
@@ -56,19 +56,29 @@
             table[r, found[m]] = jnp.int32(m)
 
 
-def prepare_kernel(p_offs, table, offs, sems):
-    fill_table(p_offs, table, offs, sems, table.shape[0], 0)
+def first_kernel(token):
+    token[...] = jnp.zeros_like(token)
 
 
-def pick_kernel(pairs, shift, table, asked, tiles, picked):
+def pick_kernel(pairs, shift, p_offs, asked, tiles, picked, found, slots, sem):
     rows, nz = tiles.shape[0], tiles.shape[1]
-    layer = lax.axis_index("layer")
+    first = lax.axis_index(GROUP) * rows
+    start = lax.rem(first, 128)
+    offs = p_offs[:, pl.ds(pl.multiple_of(first // 128 * 128, 128), 128)]
+    k = lax.broadcasted_iota(jnp.int32, offs.shape, 1) - start
+    m = lax.broadcasted_iota(jnp.int32, offs.shape, 0)
+    wanted = asked[pl.ds(lax.axis_index("layer"), 1), :]
+    for i in range(rows):
+        hit = offs == wanted[:, i : i + 1] - (k - i + shift)
+        found[i : i + 1, :] = jnp.sum(jnp.where(hit, m, 0), axis=0, keepdims=True)
+    copy = pltpu.make_async_copy(found, slots, sem)
+    copy.start()
+    copy.wait()
     for at, (i, k) in enumerate(pairs):
-        m = slot(table, k, asked[layer, i] - (k - i + shift), nz)
-        picked[at] = tiles[k, jnp.minimum(m, nz - 1)]
+        picked[at] = tiles[k, slots[i, start + k]]
 
 
-def own_kernel(p_offs, out_offs, tiles, total, left_below, left_above, table, offs, sems):
+def own_kernel(p_offs, out_offs, tiles, token, total, left_below, left_above, table, offs, sems):
     rows, nz = tiles.shape[0], tiles.shape[1]
     fill_table(p_offs, table, offs, sems, 3 * rows, rows)
     layer = lax.axis_index("layer")
@@ -111,45 +121,48 @@
     dtype = p_tiles.dtype
     p_offs, out_offs = p_offs.T, out_offs.T
     offs_scratch = [SMEM((2, nz, 128), jnp.int32), pltpu.SemaphoreType.DMA((2,))]
-    table = pl.pallas_call(
-        prepare_kernel,
-        out_shape=jax.ShapeDtypeStruct((rows, WIDTH), jnp.int32),
-        in_specs=[ANY_SPEC],
-        out_specs=SMEM_SPEC,
-        scratch_shapes=offs_scratch,
+    from_left = passed_along(out_offs, 1)
+    token = pl.pallas_call(
+        first_kernel,
+        out_shape=jax.ShapeDtypeStruct((8, 128), jnp.float32),
+        out_specs=VMEM_SPEC,
         compiler_params=LIMIT,
         cost_estimate=cost(4000, 8 << 20),
-        name="prepare",
-    )(p_offs)
-    from_left = passed_along(out_offs, 1)
-    from_right = passed_along(out_offs, -1)
-    from_left, from_right = lax.optimization_barrier((from_left, from_right))
+        name="first",
+    )()
+    mine, token = lax.optimization_barrier((out_offs, token))
+    from_right = passed_along(mine, -1)
 
     def pick(pairs, shift, wanted, name):
         return pl.pallas_call(
             lambda *refs: pick_kernel(pairs, shift, *refs),
             out_shape=jax.ShapeDtypeStruct((count, tb, tb), dtype),
-            in_specs=[SMEM_SPEC, SMEM_SPEC, VMEM_SPEC],
+            in_specs=[VMEM_SPEC, VMEM_SPEC, VMEM_SPEC],
             out_specs=VMEM_SPEC,
+            scratch_shapes=[VMEM((rows, 128), jnp.int32), SMEM((rows, 128), jnp.int32), pltpu.SemaphoreType.DMA],
             compiler_params=LIMIT,
             cost_estimate=cost(0, 2 << 20),
             name=name,
-        )(table, wanted, p_tiles)
+        )(p_offs, wanted, p_tiles)
 
-    below = passed_along(pick(BELOW, -rows, from_right, "pick_right"), 1)
-    above = passed_along(pick(ABOVE, rows, from_left, "pick_left"), -1)
+    for_left = pick(ABOVE, rows, from_left, "pick_left")
+    from_right, for_left = lax.optimization_barrier((from_right, for_left))
+    for_right = pick(BELOW, -rows, from_right, "pick_right")
+    for_right, for_left = lax.optimization_barrier((for_right, for_left))
+    below = passed_along(for_right, 1)
+    above = passed_along(for_left, -1)
     left_shape = jax.ShapeDtypeStruct((count, tb, tb), dtype)
     sum_shape = jax.ShapeDtypeStruct((rows, tb, tb), jnp.float32)
     total, left_below, left_above = pl.pallas_call(
         own_kernel,
         out_shape=(sum_shape, left_shape, left_shape),
-        in_specs=[ANY_SPEC, SMEM_SPEC, VMEM_SPEC],
+        in_specs=[ANY_SPEC, SMEM_SPEC, VMEM_SPEC, ANY_SPEC],
         out_specs=(VMEM_SPEC, VMEM_SPEC, VMEM_SPEC),
         scratch_shapes=[SMEM((3 * rows, WIDTH), jnp.int32), *offs_scratch],
         compiler_params=LIMIT,
         cost_estimate=cost(64, 8 << 20),
         name="own_rows",
-    )(p_offs, out_offs, p_tiles)
+    )(p_offs, out_offs, p_tiles, token)
 
     def halo(pairs, total, left, right, out_shape, name):
         return pl.pallas_call(

time: 61.5 us -> 58.8 us (0.956)
  Pallas kernels: 10.1 us -> 8.05 us
  local copies, waits for them, and re-layouts: 1.07 us -> 0.01 us
  starting transfers between devices: 29.4 us -> 30.2 us
    pallas_call x1, Pallas kernels: 1.98 us -> 0.01 us  [body(): pl.pallas_call(first_kernel, out_shape=jax.ShapeDtypeStruct((8, 128), jnp...]
    unnamed x6, local copies, waits for them, and re-layouts: 1.07 us -> 0.01 us
    ppermute x4, starting transfers between devices: 29.4 us -> 30.2 us  [passed_along(): return lax.ppermute(block, GROUP, route)]
  transfers between devices with their start and end apart: 4 -> 4, of which waited for: 2 -> 2; matrix products, arithmetic and copies ran while one was open for 0% -> 0% of each run, Pallas kernels for 13% -> 10%
where the time goes in v3:
time: 58.8 us; the launch traced here: 58.6 us
  starting transfers between devices  30.2 us (51%)
  waiting for transfers between devices  20.2 us (34%)
  Pallas kernels  8.05 us (14%)
    ppermute x4, starting transfers between devices, passed_along(): return lax.ppermute(block, GROUP, route)  30.2 us
    ppermute x4, waiting for transfers between devices, passed_along(): return lax.ppermute(block, GROUP, route)  20.2 us
    pallas_call x1, Pallas kernels, body(): pl.pallas_call(own_kernel, out_shape=(sum_shape, left_shape, left_shape),...  4.76 us
    pallas_call x2, Pallas kernels, halo(): pl.pallas_call(lambda *refs: halo_kernel(pairs, *refs), out_shape=out_sha...  1.65 us
    pallas_call x2, Pallas kernels, pick(): pl.pallas_call(lambda *refs: pick_kernel(pairs, shift, *refs), out_shape=...  1.64 us
  transfers between devices with their start and end apart: 4, of which 2 were waited for; matrix products, arithmetic and copies ran while one was open for 0% of the time, Pallas kernels for 10%

profile of v3, /device:TPU:1, one launch (start us, length us, event | category | flops | bytes accessed | tf_op | source)
XLA Modules:
  0.0 58.6 jit_solution(11700153279340433257)
XLA Ops:
  0.0 0.0 copy-start.2
  0.0 0.0 copy-start.1
  0.0 4.2 %collective-permute-start.1 = (s32[4,8]{1,0:T(4,128)}, s32[4,8]{1,0:T(4,128)S(1)}, u32[]{:S(2)}, u32[]{:S(2)}) collective-permute-start(s32[4,8]{1,0:T(4,128)} %bitcast.8), channel_id=1, source_target_pairs={{764,0},{0,4},{4,8},{8,12},{12,16},{16,20},{20,24},{24,28},{28,32}... | collective-permute-start | bytes 392 | tf_op jit(solution)/shard_map/ppermute | solution.py:25
  4.2 0.0 copy-start
  4.2 0.0 copy-done.2
  4.2 16.8 %collective-permute-start = (s32[4,8]{1,0:T(4,128)S(1)}, s32[4,8]{1,0:T(4,128)S(1)}, u32[]{:S(2)}, u32[]{:S(2)}) collective-permute-start(s32[4,8]{1,0:T(4,128)S(1)} %bitcast.9), channel_id=1, source_target_pairs={{4,0},{8,4},{12,8},{16,12},{20,16},{24,20},{28,24},{32,28},{36,32}... | collective-permute-start | bytes 392 | tf_op jit(solution)/shard_map/ppermute | solution.py:25
  21.0 0.0 collective-permute-done.1.refs_1_
  21.0 0.0 copy-done.1
  21.0 0.0 copy-done
  21.0 0.8 %pick_left.1 = bf16[36,128,128]{2,1,0:T(8,128)(2,1)S(1)} custom-call(s32[16,1536]{1,0:T(8,128)S(1)} %bitcast.5, s32[4,8]{1,0:T(4,128)S(1)} %collective-permute-done.1.refs_1_, bf16[8,16,128,128]{3,2,1,0:T(8,128)(2,1)S(1)} %copy-done), custom_call_target="tpu_custom_call" | custom-call | bytes 2097152 | tf_op jit(solution)/shard_map/pick_left/pallas_call | solution.py:137
  21.8 0.0 collective-permute-done.refs_1_
  21.8 0.8 %pick_right.1 = bf16[36,128,128]{2,1,0:T(8,128)(2,1)S(1)} custom-call(s32[16,1536]{1,0:T(8,128)S(1)} %bitcast.6, s32[4,8]{1,0:T(4,128)S(1)} %collective-permute-done.refs_1_, bf16[8,16,128,128]{3,2,1,0:T(8,128)(2,1)S(1)} %copy-done), custom_call_target="tpu_custom_call" | custom-call | bytes 2097152 | tf_op jit(solution)/shard_map/pick_right/pallas_call | solution.py:137
  22.7 1.9 %collective-permute-start.2 = (bf16[36,128,128]{2,1,0:T(8,128)(2,1)S(1)}, bf16[36,128,128]{2,1,0:T(8,128)(2,1)S(1)}, u32[]{:S(2)}, u32[]{:S(2)}) collective-permute-start(bf16[36,128,128]{2,1,0:T(8,128)(2,1)S(1)} %pick_right.1), channel_id=1, source_target_pairs={{764,0},{0,4},{4,8},{8,12},{12,16},{16,20},{20,24},{24,28},{28,32}... | collective-permute-start | bytes 3538952 | tf_op jit(solution)/shard_map/ppermute | solution.py:25
  24.6 7.3 %collective-permute-start.3 = (bf16[36,128,128]{2,1,0:T(8,128)(2,1)S(1)}, bf16[36,128,128]{2,1,0:T(8,128)(2,1)S(1)}, u32[]{:S(2)}, u32[]{:S(2)}) collective-permute-start(bf16[36,128,128]{2,1,0:T(8,128)(2,1)S(1)} %pick_left.1), channel_id=1, source_target_pairs={{4,0},{8,4},{12,8},{16,12},{20,16},{24,20},{28,24},{32,28},{36,32}... | collective-permute-start | bytes 3538952 | tf_op jit(solution)/shard_map/ppermute | solution.py:25
  31.9 4.8 %own_rows.1 = (f32[8,128,128]{2,1,0:T(8,128)S(1)}, bf16[36,128,128]{2,1,0:T(8,128)(2,1)S(1)}, bf16[36,128,128]{2,1,0:T(8,128)(2,1)S(1)}) custom-call(s32[16,1536]{1,0:T(8,128)S(1)} %bitcast.7, s32[4,8]{1,0:T(4,128)S(1)} %bitcast.10, bf16[8,16,128,128]{3,2,1,0:T(8,128)(2,1)S(1)} %copy-done, f32[8,128]{1,0:T(8,128)S(1)} %first.1.token), custom_call_target="tpu_custom_call" | custom-call | flops 268435456 | bytes 8388608 | tf_op jit(solution)/shard_map/own_rows/pallas_call | solution.py:156
  36.7 19.2 %collective-permute-done.2.refs_2_ = bf16[36,128,128]{2,1,0:T(8,128)(2,1)S(1)} collective-permute-done((bf16[36,128,128]{2,1,0:T(8,128)(2,1)S(1)}, bf16[36,128,128]{2,1,0:T(8,128)(2,1)S(1)}, u32[]{:S(2)}, u32[]{:S(2)}) %collective-permute-start.2) | collective-permute-done | bytes 1179680 | tf_op jit(solution)/shard_map/ppermute | solution.py:25
  55.9 0.5 rows_below.1.refs_0_
  56.4 1.0 %collective-permute-done.3.refs_2_ = bf16[36,128,128]{2,1,0:T(8,128)(2,1)S(1)} collective-permute-done((bf16[36,128,128]{2,1,0:T(8,128)(2,1)S(1)}, bf16[36,128,128]{2,1,0:T(8,128)(2,1)S(1)}, u32[]{:S(2)}, u32[]{:S(2)}) %collective-permute-start.3) | collective-permute-done | bytes 1179680 | tf_op jit(solution)/shard_map/ppermute | solution.py:25
  57.4 1.2 %rows_above.1 = bf16[8,128,128]{2,1,0:T(8,128)(2,1)} custom-call(f32[8,128,128]{2,1,0:T(8,128)S(1)} %rows_below.1.refs_0_, bf16[36,128,128]{2,1,0:T(8,128)(2,1)S(1)} %get-tuple-element.21.refs_1_, bf16[36,128,128]{2,1,0:T(8,128)(2,1)S(1)} %collective-permute-done.3.refs_2_), custom_call_target="tpu_custom_call" | custom-call | flops 150994944 | bytes 4194304 | tf_op jit(solution)/shard_map/rows_above/pallas_call | solution.py:168
  (1 shorter events, 0.0 us)
Async XLA Ops:
  0.0 4.2 %copy-start.2 = (s32[8,4]{0,1:T(4,128)S(1)}, s32[8,4]{0,1:T(4,128)}, u32[]{:S(2)}) copy-start(s32[8,4]{0,1:T(4,128)} %param.5) | copy-start | bytes 388
  0.0 21.0 %copy-start.1 = (s32[1536,16]{0,1:T(8,128)S(1)}, s32[1536,16]{0,1:T(8,128)}, u32[]{:S(2)}) copy-start(s32[1536,16]{0,1:T(8,128)} %param.4) | copy-start | bytes 294916
  0.0 21.0 %collective-permute-start.1 = (s32[4,8]{1,0:T(4,128)}, s32[4,8]{1,0:T(4,128)S(1)}, u32[]{:S(2)}, u32[]{:S(2)}) collective-permute-start(s32[4,8]{1,0:T(4,128)} %bitcast.8), channel_id=1, source_target_pairs={{764,0},{0,4},{4,8},{8,12},{12,16},{16,20},{20,24},{24,28},{28,32}... | collective-permute-start | bytes 392 | tf_op jit(solution)/shard_map/ppermute | solution.py:25
  4.2 16.8 %copy-start = (bf16[8,16,128,128]{3,2,1,0:T(8,128)(2,1)S(1)}, bf16[8,16,128,128]{3,2,1,0:T(8,128)(2,1)}, u32[]{:S(2)}) copy-start(bf16[8,16,128,128]{3,2,1,0:T(8,128)(2,1)} %refs_2_.3) | copy-start | bytes 12582916
  4.2 17.6 %collective-permute-start = (s32[4,8]{1,0:T(4,128)S(1)}, s32[4,8]{1,0:T(4,128)S(1)}, u32[]{:S(2)}, u32[]{:S(2)}) collective-permute-start(s32[4,8]{1,0:T(4,128)S(1)} %bitcast.9), channel_id=1, source_target_pairs={{4,0},{8,4},{12,8},{16,12},{20,16},{24,20},{28,24},{32,28},{36,32}... | collective-permute-start | bytes 392 | tf_op jit(solution)/shard_map/ppermute | solution.py:25
  22.7 33.3 %collective-permute-start.2 = (bf16[36,128,128]{2,1,0:T(8,128)(2,1)S(1)}, bf16[36,128,128]{2,1,0:T(8,128)(2,1)S(1)}, u32[]{:S(2)}, u32[]{:S(2)}) collective-permute-start(bf16[36,128,128]{2,1,0:T(8,128)(2,1)S(1)} %pick_right.1), channel_id=1, source_target_pairs={{764,0},{0,4},{4,8},{8,12},{12,16},{16,20},{20,24},{24,28},{28,32}... | collective-permute-start | bytes 3538952 | tf_op jit(solution)/shard_map/ppermute | solution.py:25
  24.6 32.8 %collective-permute-start.3 = (bf16[36,128,128]{2,1,0:T(8,128)(2,1)S(1)}, bf16[36,128,128]{2,1,0:T(8,128)(2,1)S(1)}, u32[]{:S(2)}, u32[]{:S(2)}) collective-permute-start(bf16[36,128,128]{2,1,0:T(8,128)(2,1)S(1)} %pick_left.1), channel_id=1, source_target_pairs={{4,0},{8,4},{12,8},{16,12},{20,16},{24,20},{28,24},{32,28},{36,32}... | collective-permute-start | bytes 3538952 | tf_op jit(solution)/shard_map/ppermute | solution.py:25
